TPU v7x, 32 devices: a whole 2x2x4 slice. The times are simulated.
32 devices in a mesh: section: 16 (over z, y, x), tp: 2 (over core).
Axes of the slice: x: 2, y: 2, z: 4, core: 2. Of those that a mesh axis runs over, the one named last changes fastest.
Arguments:
- prefill_hidden: bfloat16 [4096, 8192], P('section', 'tp'), may hold values from -180 to 180
- norm_gain: float32 [8192], replicated, may hold values from 0.25 to 1.75
- key_weight: bfloat16 [8192, 1024], P(None, 'tp'), may hold values from -0.0625 to 0.0625
- value_weight: bfloat16 [8192, 1024], P(None, 'tp'), may hold values from -0.0625 to 0.0625
- prefill_query: bfloat16 [4096, 8192], P('section', 'tp'), may hold values from -102 to 102
- resident_keys: bfloat16 [4096, 16, 1024], P('section', None, 'tp'), may hold values from -6 to 6
- resident_values: bfloat16 [4096, 16, 1024], P('section', None, 'tp'), may hold values from -6 to 6
- decode_query: bfloat16 [256, 8192], P('section', 'tp'), may hold values from -102 to 102
- page_owner: int32 [256], P('section'), may hold values from 0 to 15, as said below
- block_table: int32 [256, 62], P('section'), may hold values from 0 to 287, as said below
- context_len: int32 [256], P('section'), may hold values from 1 to 992, as said below
Outputs:
- prefill_attention: bfloat16 [4096, 8192], P('section', 'tp')
- decode_attention: bfloat16 [256, 8192], P('section', 'tp')
Inputs may be any that keep to these rules, and one draw needn't show every extreme that they name: `page_owner`: the 16 pages of each section device go to 8 different owners, exactly 2 pages to each; one owner receives pages from every section device. `block_table`: row entries name first the row's resident pages (below 256), then 256 + page_slot for at most 2 pages sent to the row's owner; every page sent to an owner is named by exactly one of its rows; entries after a row's pages are 0. `context_len`: A row's last visible token lies in the last page its table names.
All inputs are finite; a program needn't handle non-finite values.
Results may differ from a plain program's by a relative error of at most 0.011.
Values may be sent and summed in bfloat16 or wider, within the bound.
No kernel may reach another device: no remote copies, remote signals or barrier semaphores. Data moves between devices by JAX's collectives and lax.ppermute only.
A program may use at most 256 MiB of HBM per device.

v0:
```python
import functools
import math

import jax
import jax.numpy as jnp
from jax import lax
from jax.experimental import pallas as pl
from jax.experimental.pallas import tpu as pltpu
from jax.sharding import PartitionSpec as P

HD = 128
PAGE = 16
CAP = 2
CUT = 1024
NORM_EPSILON = 1e-05
ROPE_THETA = 500000.0
LOW = -1e30
EXP2_SCALE = math.log2(math.e) / math.sqrt(HD)
VMEM_BYTES = 32 * 1024 * 1024
NT = (((1,), (1,)), ((), ()))


def params(limit=VMEM_BYTES):
    return pltpu.CompilerParams(vmem_limit_bytes=limit)


def stage_kernel(n_arrays, *refs):
    copies = [
        pltpu.make_async_copy(refs[i], refs[n_arrays + i], refs[2 * n_arrays].at[i])
        for i in range(n_arrays)
    ]
    for copy in copies:
        copy.start()
    for copy in copies:
        copy.wait()


def stage(*arrays):
    return pl.pallas_call(
        functools.partial(stage_kernel, len(arrays)),
        out_shape=tuple(jax.ShapeDtypeStruct(a.shape, a.dtype) for a in arrays),
        in_specs=[pl.BlockSpec(memory_space=pl.ANY)] * len(arrays),
        out_specs=[pl.BlockSpec(memory_space=pltpu.VMEM)] * len(arrays),
        scratch_shapes=[pltpu.SemaphoreType.DMA((len(arrays),))],
        compiler_params=params(),
        cost_estimate=pl.CostEstimate(
            flops=0, bytes_accessed=sum(2 * a.size * a.dtype.itemsize for a in arrays), transcendentals=0
        ),
        name="stage",
    )(*arrays)


def project_kernel(n_parts, chunk, order_ref, *refs):
    parts = refs[:n_parts]
    gain_ref, key_ref, value_ref, cos_ref, sin_ref, column_ref, row_ref = refs[n_parts:-2]
    out_ref, total_ref = refs[-2:]
    rows, part_width = parts[0].shape
    key_width = key_ref.shape[1]
    pages = column_ref.shape[0]
    earlier = lax.broadcasted_iota(jnp.int32, (pages, pages), 1) < lax.broadcasted_iota(
        jnp.int32, (pages, pages), 0
    )
    same = earlier & (column_ref[...] == row_ref[...])
    rank = jnp.sum(same.astype(jnp.float32), axis=1, keepdims=True)
    codes = column_ref[...].astype(jnp.float32) * CAP + rank
    out_ref[rows:] = jnp.broadcast_to(codes, (pages, 2 * key_width)).astype(jnp.bfloat16)
    squares = jnp.zeros((rows, HD), jnp.float32)
    for part in parts:
        for first in range(0, part_width, HD):
            piece = part[:, first : first + HD].astype(jnp.float32)
            squares += piece * piece
    squares = jnp.sum(squares, axis=1, keepdims=True)
    inverse = lax.rsqrt(squares * (1.0 / (part_width * n_parts)) + NORM_EPSILON)
    for index, part in enumerate(parts):
        base = order_ref[index] * part_width
        for first in range(0, part_width, chunk):
            where = pl.multiple_of(base + first, chunk)
            piece = part[:, first : first + chunk].astype(jnp.float32)
            normed = (piece * inverse * gain_ref[:, pl.ds(where, chunk)]).astype(jnp.bfloat16)
            keys = jnp.dot(
                normed, key_ref[pl.ds(where, chunk)], preferred_element_type=jnp.float32
            )
            values = jnp.dot(
                normed, value_ref[pl.ds(where, chunk)], preferred_element_type=jnp.float32
            )
            if index == 0 and first == 0:
                total_ref[:, :key_width] = keys
                total_ref[:, key_width:] = values
            else:
                total_ref[:, :key_width] += keys
                total_ref[:, key_width:] += values
    for head in range(key_width // HD):
        cut = slice(head * HD, (head + 1) * HD)
        raw = total_ref[:, cut]
        turned = raw * cos_ref[...] + pltpu.roll(raw, HD // 2, 1) * sin_ref[...]
        out_ref[:rows, cut] = turned.astype(jnp.bfloat16)
    out_ref[:rows, key_width:] = total_ref[:, key_width:].astype(jnp.bfloat16)


def project(parts, order, norm_gain, key_weight, value_weight, cosine, sine, page_owner):
    rows, part_width = parts[0].shape
    n_parts = len(parts)
    key_width = key_weight.shape[1]
    vmem = pl.BlockSpec(memory_space=pltpu.VMEM)
    pages = page_owner.shape[0]
    return pl.pallas_call(
        functools.partial(project_kernel, n_parts, math.gcd(part_width, 1024)),
        out_shape=jax.ShapeDtypeStruct((rows + pages, 2 * key_width), jnp.bfloat16),
        in_specs=[pl.BlockSpec(memory_space=pltpu.SMEM)] + [vmem] * (n_parts + 7),
        out_specs=vmem,
        scratch_shapes=[pltpu.VMEM((rows, 2 * key_width), jnp.float32)],
        compiler_params=params(),
        cost_estimate=pl.CostEstimate(
            flops=4 * rows * key_width * part_width * n_parts,
            bytes_accessed=4 * key_width * part_width * n_parts,
            transcendentals=0,
        ),
        name="project",
    )(
        order,
        *parts,
        norm_gain.reshape(1, -1),
        key_weight,
        value_weight,
        cosine,
        sine,
        page_owner.reshape(-1, 1),
        page_owner.reshape(1, -1),
    )


def turned_with_ones(values):
    turned = values.T
    return jnp.concatenate([turned, jnp.ones((16, turned.shape[1]), turned.dtype)], axis=0)


def counted_piece(queries, keys, values_ones, factor, bias, old_max):
    scores = lax.dot_general(keys, queries, NT, preferred_element_type=jnp.float32)
    scores = scores * factor + bias
    new_max = jnp.maximum(old_max, jnp.max(scores, axis=0, keepdims=True))
    weights = jnp.exp2(scores - new_max).astype(jnp.bfloat16)
    product = jnp.dot(values_ones, weights, preferred_element_type=jnp.float32)
    return new_max, product


def page_bias(ids, table_ref, length, store):
    pages, lanes = ids.shape
    found = jnp.zeros((pages, lanes), jnp.int32)
    for entry in range(table_ref.shape[0]):
        left = length - entry * PAGE
        weight = jnp.where(left >= PAGE, 1, jnp.where(left > 0, CUT, 0))
        found += jnp.where(ids == table_ref[entry : entry + 1, :], weight, 0)

    def logarithm(count):
        return jnp.where(count > 0, jnp.log2(jnp.maximum(count, 1).astype(jnp.float32)), LOW)

    whole = found & (CUT - 1)
    with_cut = logarithm(whole + lax.shift_right_logical(found, CUT.bit_length() - 1))
    whole = logarithm(whole)
    token = lax.broadcasted_iota(jnp.int32, (PAGE, lanes), 0)
    kept = token < length % PAGE
    for page in range(pages):
        one = slice(page, page + 1)
        store(page, jnp.where(kept, with_cut[one], whole[one]))


def resident_kernel(
    group, pool, slot_ref, query_ref, key_ref, value_ref, table_ref, length_ref, *refs
):
    acc_ref, stat_ref, slot_bias_ref, bias = refs
    step = pl.program_id(0)
    pages, lanes = bias.shape[0] // PAGE, bias.shape[1]

    @pl.when(step == 0)
    def _():
        acc_ref[...] = jnp.zeros_like(acc_ref)
        stat_ref[:, 0:1] = jnp.full_like(stat_ref[:, 0:1], LOW)
        stat_ref[:, 1:2] = jnp.zeros_like(stat_ref[:, 1:2])
        slots = slot_bias_ref.shape[0] // PAGE
        slot_of = lax.broadcasted_iota(jnp.int32, (slots, lanes), 0)
        ids = slot_of % CAP
        for block in range(slots // CAP):
            ids += jnp.where(slot_of // CAP == block, pool + slot_ref[block] * CAP, 0)

        def store_slot(page, found):
            slot_bias_ref[page * PAGE : (page + 1) * PAGE] = found

        page_bias(ids, table_ref, length_ref[...], store_slot)

    def store(page, found):
        bias[page * PAGE : (page + 1) * PAGE] = found

    ids = step * pages + lax.broadcasted_iota(jnp.int32, (pages, lanes), 0)
    page_bias(ids, table_ref, length_ref[...], store)
    for head in range(key_ref.shape[1] // HD):
        cut = slice(head * HD, (head + 1) * HD)
        queries = jnp.concatenate(
            [
                query_ref[:, (head * group + h) * HD : (head * group + h + 1) * HD]
                for h in range(group)
            ],
            axis=0,
        )
        old_max = stat_ref[head, 0:1]
        new_max, product = counted_piece(
            queries,
            key_ref[:, cut],
            turned_with_ones(value_ref[:, cut]),
            EXP2_SCALE,
            bias[...],
            old_max,
        )
        fade = jnp.exp2(old_max - new_max)
        acc_ref[head] = acc_ref[head] * fade + product[:HD]
        stat_ref[head, 1:2] = stat_ref[head, 1:2] * fade + product[HD : HD + 1]
        stat_ref[head, 0:1] = new_max


def resident_attention(decode_query, keys, values, table, lengths, slots, pool):
    pool_rows, key_width = keys.shape
    kv_heads = key_width // HD
    group = decode_query.shape[1] // key_width
    lanes = table.shape[1]
    steps = math.gcd(pool, 4)
    chunk = pool_rows // steps

    def whole(*shape):
        return pl.BlockSpec(shape, lambda step, _: (0,) * len(shape))

    piece = pl.BlockSpec((chunk, key_width), lambda step, _: (step, 0))
    shapes = [(kv_heads, HD, lanes), (kv_heads, 8, lanes), (slots.shape[0] * CAP * PAGE, lanes)]
    return pl.pallas_call(
        functools.partial(resident_kernel, group, pool),
        out_shape=tuple(jax.ShapeDtypeStruct(shape, jnp.float32) for shape in shapes),
        grid_spec=pltpu.PrefetchScalarGridSpec(
            num_scalar_prefetch=1,
            grid=(steps,),
            in_specs=[whole(*decode_query.shape), piece, piece]
            + [whole(*table.shape), whole(*lengths.shape)],
            out_specs=[whole(*shape) for shape in shapes],
            scratch_shapes=[pltpu.VMEM((chunk, lanes), jnp.float32)],
        ),
        compiler_params=params(60 * 2**20),
        cost_estimate=pl.CostEstimate(
            flops=6 * kv_heads * lanes * pool_rows * HD,
            bytes_accessed=4 * key_width * pool_rows,
            transcendentals=kv_heads * lanes * pool_rows,
        ),
        name="resident",
    )(slots, decode_query, keys, values, table, lengths)


def pages_here(ref, head, kv_heads, own, rows, lanes):
    codes = ref[rows:, :HD].astype(jnp.float32).astype(jnp.int32)
    found = []
    for slot in range(CAP):
        mine = codes == own * CAP + slot
        both = [jnp.zeros((PAGE, HD), jnp.float32)] * 2
        for page in range(rows // PAGE):
            here = jnp.broadcast_to(mine[page : page + 1], (PAGE, HD))
            cut = slice(page * PAGE, (page + 1) * PAGE)
            both = [
                jnp.where(here, ref[cut, lanes(c)].astype(jnp.float32), held)
                for c, held in zip((head, kv_heads + head), both)
            ]
        found.append(jnp.concatenate(both, axis=1))
    return jnp.concatenate(found, axis=0).astype(jnp.bfloat16)


def attend_kernel(n_blocks, n_pages, kv_heads, group, unroll, first, final, place_ref, *refs):
    refs = list(refs)

    def take(count):
        taken, refs[:count] = refs[:count], []
        return taken

    (query_ref,) = take(1)
    blocks = take(n_blocks)
    if not first:
        acc_in, stat_in = take(2)
    if final:
        decode_ref, side_acc, side_stat, bias_ref = take(4)
        pages = take(n_pages)
        out_ref, decode_out = refs
    else:
        acc_out, stat_out, page_out = refs
    rows = query_ref.shape[0]
    own = place_ref[0]
    seen = [place_ref[1 + b] < own for b in range(n_blocks)]

    first_head = pl.program_id(0) * unroll

    def lanes(head):
        return pl.ds(pl.multiple_of(head * HD, HD), HD)

    def columns(ref, head):
        return ref[:rows, lanes(head)]

    def score(head):
        keys = jnp.concatenate([columns(ref, head) for ref in blocks], axis=0)
        queries = jnp.concatenate(
            [columns(query_ref, head * group + h) for h in range(group)], axis=0
        )
        return lax.dot_general(keys, queries, NT, preferred_element_type=jnp.float32)

    def weigh(head, scores):
        pieces = [scores[b * rows : (b + 1) * rows] for b in range(n_blocks)]
        if first:
            key_of = lax.broadcasted_iota(jnp.int32, (rows, rows), 0)
            row_of = lax.broadcasted_iota(jnp.int32, (rows, rows), 1)
            kept = jnp.concatenate([key_of <= row_of] * group, axis=1)
            pieces[0] = jnp.where(kept, pieces[0], LOW)
            new_max = jnp.max(pieces[0], axis=0, keepdims=True)
        else:
            new_max = stat_in[head, 0:1]
        for b in range(1 if first else 0, n_blocks):
            highest = jnp.max(pieces[b], axis=0, keepdims=True)
            new_max = jnp.maximum(new_max, jnp.where(seen[b], highest, LOW))
        weights = []
        for b in range(n_blocks):
            shift = new_max
            if not (first and b == 0):
                shift = new_max + jnp.where(seen[b], 0.0, -LOW)
            weights.append(jnp.exp2(pieces[b] - shift).astype(jnp.bfloat16))
        return new_max, jnp.concatenate(weights, axis=0)

    def finish(head, new_max, weights):
        values = jnp.concatenate([columns(ref, kv_heads + head) for ref in blocks], axis=0)
        product = jnp.dot(
            turned_with_ones(values), weights, preferred_element_type=jnp.float32
        )
        acc, total = product[:HD], product[HD : HD + 1]
        if not first:
            fade = jnp.exp2(stat_in[head, 0:1] - new_max)
            acc += acc_in[head] * fade
            total += stat_in[head, 1:2] * fade
        if not final:
            acc_out[head] = acc
            stat_out[head, 0:1] = new_max
            stat_out[head, 1:2] = total
            return
        result = (acc * (1.0 / total)).astype(jnp.bfloat16)
        for h in range(group):
            out_ref[:, lanes(head * group + h)] = (
                result[:, h * rows : (h + 1) * rows].T
            )

    def incoming(head):
        return jnp.concatenate(
            [pages_here(ref, head, kv_heads, own, rows, lanes) for ref in blocks], axis=0
        )

    def decode(head):
        all_pages = jnp.concatenate([ref[head] for ref in pages] + [incoming(head)], axis=0)
        decode_rows = decode_ref.shape[0]
        queries = jnp.concatenate(
            [decode_ref[:, lanes(head * group + h)] for h in range(group)], axis=0
        )
        side_max = side_stat[head, 0:1]
        new_max, product = counted_piece(
            queries,
            all_pages[:, :HD],
            turned_with_ones(all_pages[:, HD:]),
            1.0,
            bias_ref[...],
            side_max,
        )
        fade = jnp.exp2(side_max - new_max)
        acc = product[:HD] + side_acc[head] * fade
        total = product[HD : HD + 1] + side_stat[head, 1:2] * fade
        result = (acc / total).T.astype(jnp.bfloat16)
        for h in range(group):
            decode_out[:, lanes(head * group + h)] = result[h * decode_rows : (h + 1) * decode_rows]

    scores, waiting = score(first_head), None
    for index in range(unroll):
        head = first_head + index
        later = score(head + 1) if index + 1 < unroll else None
        ready = weigh(head, scores)
        if waiting is not None:
            finish(head - 1, *waiting)
        if final:
            decode(head)
        else:
            page_out[head] = incoming(head)
        scores, waiting = later, ready
    finish(first_head + unroll - 1, *waiting)


def attend(arrived, section, query, state, decode, kv_heads):
    blocks = [block for block, _ in arrived]
    place = jnp.stack([section] + [s.astype(jnp.int32) for _, s in arrived])
    n_blocks = len(blocks)
    rows, query_width = query.shape
    group = query_width // (kv_heads * HD)
    first, final = state is None, decode is not None
    total_rows = group * rows
    unroll = math.gcd(kv_heads, 2)
    vmem = pl.BlockSpec(memory_space=pltpu.VMEM)
    operands = [query, *blocks]
    held = []
    if not first:
        acc, stats, held = state
        operands += [acc, stats]
    if final:
        operands += [*decode, *held]
        out_shape = (
            jax.ShapeDtypeStruct(query.shape, jnp.bfloat16),
            jax.ShapeDtypeStruct(decode[0].shape, jnp.bfloat16),
        )
    else:
        out_shape = (
            jax.ShapeDtypeStruct((kv_heads, HD, total_rows), jnp.float32),
            jax.ShapeDtypeStruct((kv_heads, 8, total_rows), jnp.float32),
            jax.ShapeDtypeStruct((kv_heads, n_blocks * CAP * PAGE, 2 * HD), jnp.bfloat16),
        )
    pairs = kv_heads * total_rows * n_blocks * rows
    result = pl.pallas_call(
        functools.partial(
            attend_kernel, n_blocks, len(held), kv_heads, group, unroll, first, final
        ),
        out_shape=out_shape,
        grid=(kv_heads // unroll,),
        in_specs=[pl.BlockSpec(memory_space=pltpu.SMEM)] + [vmem] * len(operands),
        out_specs=[vmem] * len(out_shape),
        compiler_params=params(),
        cost_estimate=pl.CostEstimate(
            flops=6 * pairs * HD,
            bytes_accessed=12 * kv_heads * total_rows * HD,
            transcendentals=pairs,
        ),
        name="attend",
    )(place, *operands)
    if final:
        return result
    return result[0], result[1], [*held, result[2]]


def fence(*arrays):
    return lax.optimization_barrier(arrays)


def grid_sections():
    here = lax.axis_index("section")
    z, column = here // 4, here % 4
    inner = (z == 1) | (z == 2)
    plane_a = jnp.bitwise_xor(z, 1)
    plane_f = jnp.where(inner, 3 - z, jnp.where(z == 0, 2, 1))
    plane_g = jnp.where(inner, jnp.bitwise_xor(3 - z, 1), 3 - z)
    order = [(z, 0), (z, 1), (z, 2), (plane_a, 0), (z, 3), (plane_a, 2), (plane_f, 0)]
    order += [(plane_a, 1), (plane_f, 2), (plane_g, 0), (plane_f, 1), (plane_g, 2), (plane_f, 3)]
    order += [(plane_g, 1), (plane_a, 3), (plane_g, 3)]
    return [plane * 4 + jnp.bitwise_xor(column, turn) for plane, turn in order]


def gather_rounds(own, sections, work):
    sections = iter(sections)

    def named(*blocks):
        return [(block, next(sections)) for block in blocks]

    def settle(moved, work, *kept):
        return fence(*moved, *kept, *work)[: len(moved) + len(kept)]

    size_z, size_y, size_x = 4, 2, 2
    z = lax.axis_index("section") // 4

    def index(zz, yy, xx):
        return (zz * size_y + yy) * size_x + xx

    def along_z(pairs):
        return [
            (index(a, yy, xx), index(b, yy, xx))
            for a, b in pairs
            for yy in range(size_y)
            for xx in range(size_x)
        ]

    every = [(zz, yy, xx) for zz in range(size_z) for yy in range(size_y) for xx in range(size_x)]
    swap_x = [(index(zz, yy, xx), index(zz, yy, 1 - xx)) for zz, yy, xx in every]
    swap_y = [(index(zz, yy, xx), index(zz, 1 - yy, xx)) for zz, yy, xx in every]
    ends = along_z([(0, 1), (1, 0), (2, 3), (3, 2)])
    middle = along_z([(1, 2), (2, 1)])
    outward = along_z([(1, 0), (2, 3)])
    inner = (z == 1) | (z == 2)

    def move(block, pairs):
        return lax.ppermute(block, "section", pairs)

    moved = move(own, swap_x), move(own, swap_y), move(own, ends), move(own, middle)
    own_x, own_y, a, b = settle(moved, work)
    work = yield named(own, own_x, own_y, a)
    moved = move(own_y, swap_x), move(a, swap_y), move(b, outward), move(a, middle)
    own_d, a_y, c, d, a, b = settle(moved, work, a, b)
    f = jnp.where(inner, b, c)
    work = yield named(own_d, a_y, f)
    either = jnp.where(inner, d, own_d)
    moved = move(a, swap_x), move(f, swap_y), move(either, ends), move(own_d, middle)
    a_x, f_y, e, b_in, f, d = settle(moved, work, f, d)
    g = jnp.where(inner, d, e)
    work = yield named(a_x, f_y, g)
    moved = move(f, swap_x), move(g, swap_y), move(b_in, outward), move(e, middle)
    f_x, g_y, c_in, d_in, g, a_x, b_in, e = settle(moved, work, g, a_x, b_in, e)
    f_d = jnp.where(inner, b_in, c_in)
    work = yield named(f_x, g_y, f_d)
    moved = move(g, swap_x), move(a_x, swap_y), move(d_in, outward)
    g_x, a_turn, e_in = settle(moved, work)
    a_d = jnp.where(inner, e, a_turn)
    g_d = jnp.where(inner, d_in, e_in)
    yield named(g_x, a_d, g_d)


def plain_sections(section_count, section, pool):
    every = [jnp.int32(s) for s in range(section_count)]
    return [jnp.where(s == section, -pool, s) for s in every]


def gather_plain(own, section_count):
    rows = own.shape[0]
    gathered = lax.all_gather(own, "section", axis=0, tiled=True)
    step = math.gcd(section_count, 4)
    for top in range(0, section_count, step):
        yield [
            (gathered[s * rows : (s + 1) * rows], jnp.int32(s)) for s in range(top, top + step)
        ]


def per_device(
    prefill_hidden,
    norm_gain,
    key_weight,
    value_weight,
    prefill_query,
    resident_keys,
    resident_values,
    decode_query,
    page_owner,
    block_table,
    context_len,
):
    section_count = lax.axis_size("section")
    tp_count = lax.axis_size("tp")
    section = lax.axis_index("section").astype(jnp.int32)
    tp = lax.axis_index("tp").astype(jnp.int32)
    rows = prefill_hidden.shape[0]
    key_width = key_weight.shape[1]
    kv_heads = key_width // HD
    group = prefill_query.shape[1] // key_width
    pool = resident_keys.shape[0]

    if tp_count == 2:
        other = lax.ppermute(prefill_hidden, "tp", [(0, 1), (1, 0)])
        parts, order = [prefill_hidden, other], jnp.stack([tp, 1 - tp])
    else:
        parts = [lax.all_gather(prefill_hidden, "tp", axis=1, tiled=True)]
        order = jnp.zeros((1,), jnp.int32)
    half = HD // 2
    frequency = jnp.exp(jnp.arange(half, dtype=jnp.float32) * (-2.0 * math.log(ROPE_THETA) / HD))
    positions = section * rows + jnp.arange(rows, dtype=jnp.int32)
    angles = positions.astype(jnp.float32)[:, None] * frequency[None, :]
    cosine, sine = jnp.cos(angles), jnp.sin(angles)
    cosine = EXP2_SCALE * jnp.concatenate([cosine, cosine], axis=1)
    sine = EXP2_SCALE * jnp.concatenate([-sine, sine], axis=1)

    key_near, value_near = stage(key_weight, value_weight)
    own = project(
        parts, order, norm_gain, key_near, value_near, cosine, sine, page_owner
    )

    own, block_table, context_len = fence(own, block_table, context_len)
    table = jnp.concatenate([block_table] * group, axis=0).T
    lengths = jnp.concatenate([context_len] * group)[None, :]
    if section_count == 16:
        sections = grid_sections()
    else:
        sections = [section] + plain_sections(section_count, section, pool)
    decode = (
        decode_query,
        *resident_attention(
            decode_query,
            resident_keys.reshape(pool * PAGE, key_width),
            resident_values.reshape(pool * PAGE, key_width),
            table,
            lengths,
            jnp.stack(sections).astype(jnp.int32),
            pool,
        ),
    )

    def step(arrived, state, last=False):
        return attend(arrived, section, prefill_query, state, decode if last else None, kv_heads)

    if section_count == 16:
        rounds = gather_rounds(own, sections, decode[1:])
        arrived, state = next(rounds), None
        for _ in range(4):
            state = step(arrived, state)
            arrived = rounds.send((state[0], state[1]))
        return step(arrived, state, True)
    state = step([(own, section)], None)
    rounds = list(gather_plain(own, section_count))
    for arrived in rounds[:-1]:
        state = step(arrived, state)
    return step(rounds[-1], state, True)


def solution(mesh):
    return jax.shard_map(
        per_device,
        mesh=mesh,
        in_specs=(
            P("section", "tp"),
            P(),
            P(None, "tp"),
            P(None, "tp"),
            P("section", "tp"),
            P("section", None, "tp"),
            P("section", None, "tp"),
            P("section", "tp"),
            P("section"),
            P("section", None),
            P("section"),
        ),
        out_specs=(P("section", "tp"), P("section", "tp")),
        check_vma=False,
    )
```

profile of v0, /device:TPU:0, one launch (start us, length us, event | category | flops | bytes accessed | tf_op | source)
XLA Modules:
  0.0 113.7 jit_solution(3802520488953829628)
XLA Ops:
  0.6 0.5 collective-permute-start
  1.1 0.7 copy.13.refs_7_
  1.9 5.9 %stage.1 = (bf16[8192,512]{1,0:T(8,128)(2,1)S(1)}, bf16[8192,512]{1,0:T(8,128)(2,1)S(1)}) custom-call(bf16[8192,512]{1,0:T(8,128)(2,1)} %refs_0_.7, bf16[8192,512]{1,0:T(8,128)(2,1)} %refs_1_.1), custom_call_target="tpu_custom_call" | custom-call | bytes 33554432 | tf_op jit(solution)/shard_map/stage/pallas_call | solution.py:39
  7.8 0.1 pad_add_fusion.1.order_ref
  7.9 0.5 fusion
  8.5 0.1 maximum_multiply_fusion
  8.7 5.9 %project.1.refs_1_ = bf16[272,1024]{1,0:T(8,128)(2,1)S(1)} custom-call(s32[2]{0:T(128)S(1)} %pad_add_fusion.1.order_ref, bf16[256,4096]{1,0:T(8,128)(2,1)S(1)} %copy-done, bf16[256,4096]{1,0:T(8,128)(2,1)S(1)} %collective-permute-done.refs_1_, f32[1,8192]{1,0:T(1,128)S(1)} %bitcast.26, bf16[8192,512]{1,0:T(8,128)(2,1)S(1)} %get-tuple-element.49.refs_3_, ...), custom_call_target="tpu_custom_call" | custom-call | flops 4294967296 | bytes 16777216 | tf_op jit(solution)/shard_map/project/pallas_call | solution.py:106
  14.6 0.7 collective-permute-start.4
  15.3 5.5 %collective-permute-start.3 = (bf16[272,1024]{1,0:T(8,128)(2,1)S(1)}, bf16[272,1024]{1,0:T(8,128)(2,1)S(1)}, u32[]{:S(2)}, u32[]{:S(2)}) collective-permute-start(bf16[272,1024]{1,0:T(8,128)(2,1)S(1)} %project.1.refs_1_), channel_id=1, source_target_pairs={{0,8},{2,10},{4,12},{6,14},{8,0},{10,2},{12,4},{14,6},{16,24},{18,... | collective-permute-start | bytes 1671176 | tf_op jit(solution)/shard_map/ppermute | solution.py:488
  20.8 1.5 %collective-permute-start.2 = (bf16[272,1024]{1,0:T(8,128)(2,1)S(1)}, bf16[272,1024]{1,0:T(8,128)(2,1)S(1)}, u32[]{:S(2)}, u32[]{:S(2)}) collective-permute-start(bf16[272,1024]{1,0:T(8,128)(2,1)S(1)} %project.1.refs_1_), channel_id=1, source_target_pairs={{0,4},{2,6},{4,0},{6,2},{8,12},{10,14},{12,8},{14,10},{16,20},{18,... | collective-permute-start | bytes 1671176 | tf_op jit(solution)/shard_map/ppermute | solution.py:488
  22.3 1.5 %collective-permute-start.1 = (bf16[272,1024]{1,0:T(8,128)(2,1)S(1)}, bf16[272,1024]{1,0:T(8,128)(2,1)S(1)}, u32[]{:S(2)}, u32[]{:S(2)}) collective-permute-start(bf16[272,1024]{1,0:T(8,128)(2,1)S(1)} %project.1.refs_1_), channel_id=1, source_target_pairs={{0,2},{2,0},{4,6},{6,4},{8,10},{10,8},{12,14},{14,12},{16,18},{18,... | collective-permute-start | bytes 1671176 | tf_op jit(solution)/shard_map/ppermute | solution.py:488
  23.8 0.1 stack.120.place_ref
  23.9 0.7 stack.119.slot_ref
  24.6 0.1 pad_add_fusion.2
  24.6 0.7 concatenate.15
  25.3 0.1 copy.14
  25.4 0.7 concatenate.14
  26.2 8.8 %resident.1 = (f32[4,128,128]{2,1,0:T(8,128)}, f32[4,8,128]{2,1,0:T(8,128)}, f32[512,128]{1,0:T(8,128)}) custom-call(s32[16]{0:T(128)} %stack.119.slot_ref, bf16[16,4096]{1,0:T(8,128)(2,1)} %refs_6_.1, bf16[4096,512]{1,0:T(8,128)(2,1)} %bitcast.29, bf16[4096,512]{1,0:T(8,128)(2,1)} %bitcast.30, s32[62,128]{1,0:T(8,128)} %bitcast.31, s32[1,128]{1,0:T(1,128)} %bitcast.32), custom_call_target="tpu_custom_call" | custom-call | flops 1610612736 | bytes 8388608 | tf_op jit(solution)/shard_map/resident/pallas_call | solution.py:232
  34.9 0.3 collective-permute-done.2.refs_3_
  35.2 1.2 %collective-permute-done.1.refs_2_ = bf16[272,1024]{1,0:T(8,128)(2,1)S(1)} collective-permute-done((bf16[272,1024]{1,0:T(8,128)(2,1)S(1)}, bf16[272,1024]{1,0:T(8,128)(2,1)S(1)}, u32[]{:S(2)}, u32[]{:S(2)}) %collective-permute-start.1) | collective-permute-done | bytes 557088 | tf_op jit(solution)/shard_map/ppermute | solution.py:488
  36.5 0.7 collective-permute-start.8
  37.2 0.6 collective-permute-start.6
  37.7 1.5 %collective-permute-start.5 = (bf16[272,1024]{1,0:T(8,128)(2,1)S(1)}, bf16[272,1024]{1,0:T(8,128)(2,1)S(1)}, u32[]{:S(2)}, u32[]{:S(2)}) collective-permute-start(bf16[272,1024]{1,0:T(8,128)(2,1)S(1)} %collective-permute-done.2.refs_3_), channel_id=1, source_target_pairs={{0,2},{2,0},{4,6},{6,4},{8,10},{10,8},{12,14},{14,12},{16,18},{18,... | collective-permute-start | bytes 1671176 | tf_op jit(solution)/shard_map/ppermute | solution.py:488
  39.2 1.5 %collective-permute-start.7 = (bf16[272,1024]{1,0:T(8,128)(2,1)S(1)}, bf16[272,1024]{1,0:T(8,128)(2,1)S(1)}, u32[]{:S(2)}, u32[]{:S(2)}) collective-permute-start(bf16[272,1024]{1,0:T(8,128)(2,1)S(1)} %collective-permute-done.4), channel_id=1, source_target_pairs={{8,0},{10,2},{12,4},{14,6},{16,24},{18,26},{20,28},{22,30},{9,1},{... | collective-permute-start | bytes 1671176 | tf_op jit(solution)/shard_map/ppermute | solution.py:488
  40.7 1.6 %copy-done.4 = bf16[256,4096]{1,0:T(8,128)(2,1)S(1)} copy-done((bf16[256,4096]{1,0:T(8,128)(2,1)S(1)}, bf16[256,4096]{1,0:T(8,128)(2,1)}, u32[]{:S(2)}) %copy-start.4) | copy-done | bytes 2097176
  42.3 10.8 %attend.5 = (f32[4,128,2048]{2,1,0:T(8,128)S(1)}, f32[4,8,2048]{2,1,0:T(8,128)S(1)}, bf16[4,128,256]{2,1,0:T(8,128)(2,1)S(1)}) custom-call(s32[5]{0:T(128)S(1)} %stack.120.place_ref, bf16[256,4096]{1,0:T(8,128)(2,1)S(1)} %copy-done.4, bf16[272,1024]{1,0:T(8,128)(2,1)S(1)} %project.1.refs_1_, bf16[272,1024]{1,0:T(8,128)(2,1)S(1)} %collective-permute-done.1.refs_2_, ...), custom_call_target="tpu_custom_call" | custom-call | flops 6442450944 | bytes 12582912 | tf_op jit(solution)/shard_map/attend/pallas_call | solution.py:418
  53.1 0.8 collective-permute-done.7
  54.0 0.7 collective-permute-start.12
  54.7 4.1 %collective-permute-start.11 = (bf16[272,1024]{1,0:T(8,128)(2,1)S(1)}, bf16[272,1024]{1,0:T(8,128)(2,1)S(1)}, u32[]{:S(2)}, u32[]{:S(2)}) collective-permute-start(bf16[272,1024]{1,0:T(8,128)(2,1)S(1)} %broadcast_select_fusion.4), channel_id=1, source_target_pairs={{0,8},{2,10},{4,12},{6,14},{8,0},{10,2},{12,4},{14,6},{16,24},{18,... | collective-permute-start | bytes 1671176 | tf_op jit(solution)/shard_map/ppermute | solution.py:488
  58.8 0.1 broadcast_select_fusion.5.refs_3_
  58.9 1.6 %collective-permute-start.10 = (bf16[272,1024]{1,0:T(8,128)(2,1)S(1)}, bf16[272,1024]{1,0:T(8,128)(2,1)S(1)}, u32[]{:S(2)}, u32[]{:S(2)}) collective-permute-start(bf16[272,1024]{1,0:T(8,128)(2,1)S(1)} %broadcast_select_fusion.5.refs_3_), channel_id=1, source_target_pairs={{0,4},{2,6},{4,0},{6,2},{8,12},{10,14},{12,8},{14,10},{16,20},{18,... | collective-permute-start | bytes 1671176 | tf_op jit(solution)/shard_map/ppermute | solution.py:488
  60.5 0.5 collective-permute-start.9
  61.1 9.1 %attend.6 = (f32[4,128,2048]{2,1,0:T(8,128)S(1)}, f32[4,8,2048]{2,1,0:T(8,128)S(1)}, bf16[4,96,256]{2,1,0:T(8,128)(2,1)S(1)}) custom-call(s32[4]{0:T(128)S(1)} %get-tuple-element.99.place_ref, bf16[256,4096]{1,0:T(8,128)(2,1)S(1)} %copy-done.4, bf16[272,1024]{1,0:T(8,128)(2,1)S(1)} %collective-permute-done.5.refs_1_, ...), custom_call_target="tpu_custom_call" | custom-call | flops 4831838208 | bytes 12582912 | tf_op jit(solution)/shard_map/attend/pallas_call | solution.py:418
  70.2 1.1 collective-permute-done.10.refs_2_
  71.3 1.1 %collective-permute-done.9.refs_1_ = bf16[272,1024]{1,0:T(8,128)(2,1)S(1)} collective-permute-done((bf16[272,1024]{1,0:T(8,128)(2,1)S(1)}, bf16[272,1024]{1,0:T(8,128)(2,1)S(1)}, u32[]{:S(2)}, u32[]{:S(2)}) %collective-permute-start.9) | collective-permute-done | bytes 557088 | tf_op jit(solution)/shard_map/ppermute | solution.py:488
  72.5 0.7 collective-permute-start.16
  73.2 0.7 collective-permute-start.14
  73.9 0.5 collective-permute-start.13
  74.4 1.5 %collective-permute-start.15 = (bf16[272,1024]{1,0:T(8,128)(2,1)S(1)}, bf16[272,1024]{1,0:T(8,128)(2,1)S(1)}, u32[]{:S(2)}, u32[]{:S(2)}) collective-permute-start(bf16[272,1024]{1,0:T(8,128)(2,1)S(1)} %collective-permute-done.12), channel_id=1, source_target_pairs={{8,0},{10,2},{12,4},{14,6},{16,24},{18,26},{20,28},{22,30},{9,1},{... | collective-permute-start | bytes 1671176 | tf_op jit(solution)/shard_map/ppermute | solution.py:488
  75.9 0.1 pad_add_fusion.place_ref
  76.0 9.2 %attend.7 = (f32[4,128,2048]{2,1,0:T(8,128)S(1)}, f32[4,8,2048]{2,1,0:T(8,128)S(1)}, bf16[4,96,256]{2,1,0:T(8,128)(2,1)S(1)}) custom-call(s32[4]{0:T(128)S(1)} %get-tuple-element.100.place_ref, bf16[256,4096]{1,0:T(8,128)(2,1)S(1)} %copy-done.4, bf16[272,1024]{1,0:T(8,128)(2,1)S(1)} %collective-permute-done.9.refs_1_, ...), custom_call_target="tpu_custom_call" | custom-call | flops 4831838208 | bytes 12582912 | tf_op jit(solution)/shard_map/attend/pallas_call | solution.py:418
  85.2 1.6 %collective-permute-done.15 = bf16[272,1024]{1,0:T(8,128)(2,1)S(1)} collective-permute-done((bf16[272,1024]{1,0:T(8,128)(2,1)S(1)}, bf16[272,1024]{1,0:T(8,128)(2,1)S(1)}, u32[]{:S(2)}, u32[]{:S(2)}) %collective-permute-start.15) | collective-permute-done | bytes 557088 | tf_op jit(solution)/shard_map/ppermute | solution.py:488
  86.8 1.6 %collective-permute-start.17 = (bf16[272,1024]{1,0:T(8,128)(2,1)S(1)}, bf16[272,1024]{1,0:T(8,128)(2,1)S(1)}, u32[]{:S(2)}, u32[]{:S(2)}) collective-permute-start(bf16[272,1024]{1,0:T(8,128)(2,1)S(1)} %broadcast_select_fusion.3.refs_3_), channel_id=1, source_target_pairs={{0,2},{2,0},{4,6},{6,4},{8,10},{10,8},{12,14},{14,12},{16,18},{18,... | collective-permute-start | bytes 1671176 | tf_op jit(solution)/shard_map/ppermute | solution.py:488
  88.4 1.3 %collective-permute-start.18 = (bf16[272,1024]{1,0:T(8,128)(2,1)S(1)}, bf16[272,1024]{1,0:T(8,128)(2,1)S(1)}, u32[]{:S(2)}, u32[]{:S(2)}) collective-permute-start(bf16[272,1024]{1,0:T(8,128)(2,1)S(1)} %collective-permute-done.9.refs_1_), channel_id=1, source_target_pairs={{0,4},{2,6},{4,0},{6,2},{8,12},{10,14},{12,8},{14,10},{16,20},{18,... | collective-permute-start | bytes 1671176 | tf_op jit(solution)/shard_map/ppermute | solution.py:488
  89.7 1.3 %collective-permute-start.19 = (bf16[272,1024]{1,0:T(8,128)(2,1)S(1)}, bf16[272,1024]{1,0:T(8,128)(2,1)S(1)}, u32[]{:S(2)}, u32[]{:S(2)}) collective-permute-start(bf16[272,1024]{1,0:T(8,128)(2,1)S(1)} %collective-permute-done.16), channel_id=1, source_target_pairs={{8,0},{10,2},{12,4},{14,6},{16,24},{18,26},{20,28},{22,30},{9,1},{... | collective-permute-start | bytes 1671176 | tf_op jit(solution)/shard_map/ppermute | solution.py:488
  91.1 9.1 %attend.8 = (f32[4,128,2048]{2,1,0:T(8,128)S(1)}, f32[4,8,2048]{2,1,0:T(8,128)S(1)}, bf16[4,96,256]{2,1,0:T(8,128)(2,1)S(1)}) custom-call(s32[4]{0:T(128)S(1)} %pad_add_fusion.4.place_ref, bf16[256,4096]{1,0:T(8,128)(2,1)S(1)} %copy-done.4, bf16[272,1024]{1,0:T(8,128)(2,1)S(1)} %collective-permute-done.13.refs_1_, ...), custom_call_target="tpu_custom_call" | custom-call | flops 4831838208 | bytes 12582912 | tf_op jit(solution)/shard_map/attend/pallas_call | solution.py:418
  100.2 0.9 collective-permute-done.19
  101.3 12.4 %attend.9 = (bf16[256,4096]{1,0:T(8,128)(2,1)}, bf16[16,4096]{1,0:T(8,128)(2,1)}) custom-call(s32[4]{0:T(128)S(1)} %pad_add_fusion.place_ref, bf16[256,4096]{1,0:T(8,128)(2,1)S(1)} %copy-done.4, bf16[272,1024]{1,0:T(8,128)(2,1)S(1)} %collective-permute-done.17.refs_1_, bf16[272,1024]{1,0:T(8,128)(2,1)S(1)} %broadcast_select_fusion.1.refs_2_, ...), custom_call_target="tpu_custom_call" | custom-call | flops 4831838208 | bytes 12582912 | tf_op jit(solution)/shard_map/attend/pallas_call | solution.py:418
  (40 shorter events, 0.5 us)
Async XLA Ops:
  0.6 8.0 %collective-permute-start = (bf16[256,4096]{1,0:T(8,128)(2,1)}, bf16[256,4096]{1,0:T(8,128)(2,1)S(1)}, u32[]{:S(2)}, u32[]{:S(2)}) collective-permute-start(bf16[256,4096]{1,0:T(8,128)(2,1)} %refs_0_.8), channel_id=1, source_target_pairs={{0,1},{1,0},{2,3},{3,2},{4,5},{5,4},{6,7},{7,6},{8,9},{9,8},{10,11... | collective-permute-start | bytes 6291464 | tf_op jit(solution)/shard_map/ppermute | solution.py:552
  1.9 6.7 %copy-start = (bf16[256,4096]{1,0:T(8,128)(2,1)S(1)}, bf16[256,4096]{1,0:T(8,128)(2,1)}, u32[]{:S(2)}) copy-start(bf16[256,4096]{1,0:T(8,128)(2,1)} %refs_0_.8) | copy-start | bytes 6291460
  1.9 6.8 %copy-start.2 = (f32[8192]{0:T(1024)S(1)}, f32[8192]{0:T(1024)}, u32[]{:S(2)}) copy-start(f32[8192]{0:T(1024)} %param.12) | copy-start | bytes 98308
  1.9 6.8 %copy-start.3 = (s32[16]{0:T(128)S(1)}, s32[16]{0:T(128)}, u32[]{:S(2)}) copy-start(s32[16]{0:T(128)} %param.19) | copy-start | bytes 196
  8.7 16.0 %copy-start.8 = (s32[16]{0:T(128)S(1)}, s32[16]{0:T(128)}, u32[]{:S(2)}) copy-start(s32[16]{0:T(128)} %param.21) | copy-start | bytes 196
  8.7 16.7 %copy-start.9 = (s32[16,62]{1,0:T(8,128)S(1)}, s32[16,62]{1,0:T(8,128)}, u32[]{:S(2)}) copy-start(s32[16,62]{1,0:T(8,128)} %param.20) | copy-start | bytes 11908
  14.6 20.3 %collective-permute-start.4 = (bf16[272,1024]{1,0:T(8,128)(2,1)S(1)}, bf16[272,1024]{1,0:T(8,128)(2,1)S(1)}, u32[]{:S(2)}, u32[]{:S(2)}) collective-permute-start(bf16[272,1024]{1,0:T(8,128)(2,1)S(1)} %project.1.refs_1_), channel_id=1, source_target_pairs={{8,16},{10,18},{12,20},{14,22},{16,8},{18,10},{20,12},{22,14},{9,1... | collective-permute-start | bytes 1671176 | tf_op jit(solution)/shard_map/ppermute | solution.py:488
  15.3 19.6 %collective-permute-start.3 = (bf16[272,1024]{1,0:T(8,128)(2,1)S(1)}, bf16[272,1024]{1,0:T(8,128)(2,1)S(1)}, u32[]{:S(2)}, u32[]{:S(2)}) collective-permute-start(bf16[272,1024]{1,0:T(8,128)(2,1)S(1)} %project.1.refs_1_), channel_id=1, source_target_pairs={{0,8},{2,10},{4,12},{6,14},{8,0},{10,2},{12,4},{14,6},{16,24},{18,... | collective-permute-start | bytes 1671176 | tf_op jit(solution)/shard_map/ppermute | solution.py:488
  20.8 14.5 %collective-permute-start.2 = (bf16[272,1024]{1,0:T(8,128)(2,1)S(1)}, bf16[272,1024]{1,0:T(8,128)(2,1)S(1)}, u32[]{:S(2)}, u32[]{:S(2)}) collective-permute-start(bf16[272,1024]{1,0:T(8,128)(2,1)S(1)} %project.1.refs_1_), channel_id=1, source_target_pairs={{0,4},{2,6},{4,0},{6,2},{8,12},{10,14},{12,8},{14,10},{16,20},{18,... | collective-permute-start | bytes 1671176 | tf_op jit(solution)/shard_map/ppermute | solution.py:488
  22.3 14.2 %collective-permute-start.1 = (bf16[272,1024]{1,0:T(8,128)(2,1)S(1)}, bf16[272,1024]{1,0:T(8,128)(2,1)S(1)}, u32[]{:S(2)}, u32[]{:S(2)}) collective-permute-start(bf16[272,1024]{1,0:T(8,128)(2,1)S(1)} %project.1.refs_1_), channel_id=1, source_target_pairs={{0,2},{2,0},{4,6},{6,4},{8,10},{10,8},{12,14},{14,12},{16,18},{18,... | collective-permute-start | bytes 1671176 | tf_op jit(solution)/shard_map/ppermute | solution.py:488
  36.5 17.5 %collective-permute-start.8 = (bf16[272,1024]{1,0:T(8,128)(2,1)S(1)}, bf16[272,1024]{1,0:T(8,128)(2,1)S(1)}, u32[]{:S(2)}, u32[]{:S(2)}) collective-permute-start(bf16[272,1024]{1,0:T(8,128)(2,1)S(1)} %collective-permute-done.3.refs_4_), channel_id=1, source_target_pairs={{8,16},{10,18},{12,20},{14,22},{16,8},{18,10},{20,12},{22,14},{9,1... | collective-permute-start | bytes 1671176 | tf_op jit(solution)/shard_map/ppermute | solution.py:488
  37.2 16.8 %collective-permute-start.6 = (bf16[272,1024]{1,0:T(8,128)(2,1)S(1)}, bf16[272,1024]{1,0:T(8,128)(2,1)S(1)}, u32[]{:S(2)}, u32[]{:S(2)}) collective-permute-start(bf16[272,1024]{1,0:T(8,128)(2,1)S(1)} %collective-permute-done.3.refs_4_), channel_id=1, source_target_pairs={{0,4},{2,6},{4,0},{6,2},{8,12},{10,14},{12,8},{14,10},{16,20},{18,... | collective-permute-start | bytes 1671176 | tf_op jit(solution)/shard_map/ppermute | solution.py:488
  37.7 15.4 %collective-permute-start.5 = (bf16[272,1024]{1,0:T(8,128)(2,1)S(1)}, bf16[272,1024]{1,0:T(8,128)(2,1)S(1)}, u32[]{:S(2)}, u32[]{:S(2)}) collective-permute-start(bf16[272,1024]{1,0:T(8,128)(2,1)S(1)} %collective-permute-done.2.refs_3_), channel_id=1, source_target_pairs={{0,2},{2,0},{4,6},{6,4},{8,10},{10,8},{12,14},{14,12},{16,18},{18,... | collective-permute-start | bytes 1671176 | tf_op jit(solution)/shard_map/ppermute | solution.py:488
  39.2 14.7 %collective-permute-start.7 = (bf16[272,1024]{1,0:T(8,128)(2,1)S(1)}, bf16[272,1024]{1,0:T(8,128)(2,1)S(1)}, u32[]{:S(2)}, u32[]{:S(2)}) collective-permute-start(bf16[272,1024]{1,0:T(8,128)(2,1)S(1)} %collective-permute-done.4), channel_id=1, source_target_pairs={{8,0},{10,2},{12,4},{14,6},{16,24},{18,26},{20,28},{22,30},{9,1},{... | collective-permute-start | bytes 1671176 | tf_op jit(solution)/shard_map/ppermute | solution.py:488
  40.7 1.6 %copy-start.4 = (bf16[256,4096]{1,0:T(8,128)(2,1)S(1)}, bf16[256,4096]{1,0:T(8,128)(2,1)}, u32[]{:S(2)}) copy-start(bf16[256,4096]{1,0:T(8,128)(2,1)} %refs_0_.13) | copy-start | bytes 6291460
  54.0 18.5 %collective-permute-start.12 = (bf16[272,1024]{1,0:T(8,128)(2,1)S(1)}, bf16[272,1024]{1,0:T(8,128)(2,1)S(1)}, u32[]{:S(2)}, u32[]{:S(2)}) collective-permute-start(bf16[272,1024]{1,0:T(8,128)(2,1)S(1)} %collective-permute-done.5.refs_1_), channel_id=1, source_target_pairs={{8,16},{10,18},{12,20},{14,22},{16,8},{18,10},{20,12},{22,14},{9,1... | collective-permute-start | bytes 1671176 | tf_op jit(solution)/shard_map/ppermute | solution.py:488
  54.7 15.5 %collective-permute-start.11 = (bf16[272,1024]{1,0:T(8,128)(2,1)S(1)}, bf16[272,1024]{1,0:T(8,128)(2,1)S(1)}, u32[]{:S(2)}, u32[]{:S(2)}) collective-permute-start(bf16[272,1024]{1,0:T(8,128)(2,1)S(1)} %broadcast_select_fusion.4), channel_id=1, source_target_pairs={{0,8},{2,10},{4,12},{6,14},{8,0},{10,2},{12,4},{14,6},{16,24},{18,... | collective-permute-start | bytes 1671176 | tf_op jit(solution)/shard_map/ppermute | solution.py:488
  58.9 12.4 %collective-permute-start.10 = (bf16[272,1024]{1,0:T(8,128)(2,1)S(1)}, bf16[272,1024]{1,0:T(8,128)(2,1)S(1)}, u32[]{:S(2)}, u32[]{:S(2)}) collective-permute-start(bf16[272,1024]{1,0:T(8,128)(2,1)S(1)} %broadcast_select_fusion.5.refs_3_), channel_id=1, source_target_pairs={{0,4},{2,6},{4,0},{6,2},{8,12},{10,14},{12,8},{14,10},{16,20},{18,... | collective-permute-start | bytes 1671176 | tf_op jit(solution)/shard_map/ppermute | solution.py:488
  60.5 11.9 %collective-permute-start.9 = (bf16[272,1024]{1,0:T(8,128)(2,1)S(1)}, bf16[272,1024]{1,0:T(8,128)(2,1)S(1)}, u32[]{:S(2)}, u32[]{:S(2)}) collective-permute-start(bf16[272,1024]{1,0:T(8,128)(2,1)S(1)} %collective-permute-done.3.refs_4_), channel_id=1, source_target_pairs={{0,2},{2,0},{4,6},{6,4},{8,10},{10,8},{12,14},{14,12},{16,18},{18,... | collective-permute-start | bytes 1671176 | tf_op jit(solution)/shard_map/ppermute | solution.py:488
  72.5 14.3 %collective-permute-start.16 = (bf16[272,1024]{1,0:T(8,128)(2,1)S(1)}, bf16[272,1024]{1,0:T(8,128)(2,1)S(1)}, u32[]{:S(2)}, u32[]{:S(2)}) collective-permute-start(bf16[272,1024]{1,0:T(8,128)(2,1)S(1)} %collective-permute-done.11), channel_id=1, source_target_pairs={{8,16},{10,18},{12,20},{14,22},{16,8},{18,10},{20,12},{22,14},{9,1... | collective-permute-start | bytes 1671176 | tf_op jit(solution)/shard_map/ppermute | solution.py:488
  73.2 12.0 %collective-permute-start.14 = (bf16[272,1024]{1,0:T(8,128)(2,1)S(1)}, bf16[272,1024]{1,0:T(8,128)(2,1)S(1)}, u32[]{:S(2)}, u32[]{:S(2)}) collective-permute-start(bf16[272,1024]{1,0:T(8,128)(2,1)S(1)} %broadcast_select_fusion.3.refs_3_), channel_id=1, source_target_pairs={{0,4},{2,6},{4,0},{6,2},{8,12},{10,14},{12,8},{14,10},{16,20},{18,... | collective-permute-start | bytes 1671176 | tf_op jit(solution)/shard_map/ppermute | solution.py:488
  73.9 11.3 %collective-permute-start.13 = (bf16[272,1024]{1,0:T(8,128)(2,1)S(1)}, bf16[272,1024]{1,0:T(8,128)(2,1)S(1)}, u32[]{:S(2)}, u32[]{:S(2)}) collective-permute-start(bf16[272,1024]{1,0:T(8,128)(2,1)S(1)} %broadcast_select_fusion.5.refs_3_), channel_id=1, source_target_pairs={{0,2},{2,0},{4,6},{6,4},{8,10},{10,8},{12,14},{14,12},{16,18},{18,... | collective-permute-start | bytes 1671176 | tf_op jit(solution)/shard_map/ppermute | solution.py:488
  74.4 12.4 %collective-permute-start.15 = (bf16[272,1024]{1,0:T(8,128)(2,1)S(1)}, bf16[272,1024]{1,0:T(8,128)(2,1)S(1)}, u32[]{:S(2)}, u32[]{:S(2)}) collective-permute-start(bf16[272,1024]{1,0:T(8,128)(2,1)S(1)} %collective-permute-done.12), channel_id=1, source_target_pairs={{8,0},{10,2},{12,4},{14,6},{16,24},{18,26},{20,28},{22,30},{9,1},{... | collective-permute-start | bytes 1671176 | tf_op jit(solution)/shard_map/ppermute | solution.py:488
  86.8 13.4 %collective-permute-start.17 = (bf16[272,1024]{1,0:T(8,128)(2,1)S(1)}, bf16[272,1024]{1,0:T(8,128)(2,1)S(1)}, u32[]{:S(2)}, u32[]{:S(2)}) collective-permute-start(bf16[272,1024]{1,0:T(8,128)(2,1)S(1)} %broadcast_select_fusion.3.refs_3_), channel_id=1, source_target_pairs={{0,2},{2,0},{4,6},{6,4},{8,10},{10,8},{12,14},{14,12},{16,18},{18,... | collective-permute-start | bytes 1671176 | tf_op jit(solution)/shard_map/ppermute | solution.py:488
  88.4 11.8 %collective-permute-start.18 = (bf16[272,1024]{1,0:T(8,128)(2,1)S(1)}, bf16[272,1024]{1,0:T(8,128)(2,1)S(1)}, u32[]{:S(2)}, u32[]{:S(2)}) collective-permute-start(bf16[272,1024]{1,0:T(8,128)(2,1)S(1)} %collective-permute-done.9.refs_1_), channel_id=1, source_target_pairs={{0,4},{2,6},{4,0},{6,2},{8,12},{10,14},{12,8},{14,10},{16,20},{18,... | collective-permute-start | bytes 1671176 | tf_op jit(solution)/shard_map/ppermute | solution.py:488
  89.7 11.4 %collective-permute-start.19 = (bf16[272,1024]{1,0:T(8,128)(2,1)S(1)}, bf16[272,1024]{1,0:T(8,128)(2,1)S(1)}, u32[]{:S(2)}, u32[]{:S(2)}) collective-permute-start(bf16[272,1024]{1,0:T(8,128)(2,1)S(1)} %collective-permute-done.16), channel_id=1, source_target_pairs={{8,0},{10,2},{12,4},{14,6},{16,24},{18,26},{20,28},{22,30},{9,1},{... | collective-permute-start | bytes 1671176 | tf_op jit(solution)/shard_map/ppermute | solution.py:488
  91.0 10.2 %copy-start.1 = (bf16[16,4096]{1,0:T(8,128)(2,1)S(1)}, bf16[16,4096]{1,0:T(8,128)(2,1)}, u32[]{:S(2)}) copy-start(bf16[16,4096]{1,0:T(8,128)(2,1)} %refs_6_.1) | copy-start | bytes 393220
  91.1 10.2 %copy-start.5 = (f32[4,128,128]{2,1,0:T(8,128)S(1)}, f32[4,128,128]{2,1,0:T(8,128)}, u32[]{:S(2)}) copy-start(f32[4,128,128]{2,1,0:T(8,128)} %get-tuple-element.54.refs_7_) | copy-start | bytes 786436
  91.1 10.2 %copy-start.6 = (f32[512,128]{1,0:T(8,128)S(1)}, f32[512,128]{1,0:T(8,128)}, u32[]{:S(2)}) copy-start(f32[512,128]{1,0:T(8,128)} %get-tuple-element.56.refs_9_) | copy-start | bytes 786436
  91.1 10.2 %copy-start.7 = (f32[4,8,128]{2,1,0:T(8,128)S(1)}, f32[4,8,128]{2,1,0:T(8,128)}, u32[]{:S(2)}) copy-start(f32[4,8,128]{2,1,0:T(8,128)} %get-tuple-element.55.refs_8_) | copy-start | bytes 49156
where the time goes:
time: 114 us
  Pallas kernels  71.2 us (62%)
  starting transfers between devices  28.3 us (25%)
  waiting for transfers between devices  7.16 us (6%)
  local copies, waits for them, and re-layouts  4.65 us (4%)
  other arithmetic  1.38 us (1%)
    pallas_call x5, Pallas kernels, attend(): pl.pallas_call(functools.partial(attend_kernel, n_blocks, len(held), kv_h...  50.6 us
    ppermute x19, starting transfers between devices, move(): return lax.ppermute(block, 'section', pairs)  27.8 us
    pallas_call x1, Pallas kernels, resident_attention(): pl.pallas_call(functools.partial(resident_kernel, group, pool), out_shape...  8.75 us
    ppermute x19, waiting for transfers between devices, move(): return lax.ppermute(block, 'section', pairs)  7.15 us
    pallas_call x1, Pallas kernels, project(): pl.pallas_call(functools.partial(project_kernel, n_parts, math.gcd(part_w...  5.95 us
    pallas_call x1, Pallas kernels, stage(): pl.pallas_call(functools.partial(stage_kernel, len(arrays)), out_shape=tu...  5.93 us
  transfers between devices with their start and end apart: 20, of which 7 were waited for; matrix products, arithmetic and copies ran while one was open for 4% of the time, Pallas kernels for 46%

commit v1 on v0

--- a/solution.py
+++ b/solution.py
@@ -52,17 +52,18 @@
 
 def project_kernel(n_parts, chunk, order_ref, *refs):
     parts = refs[:n_parts]
-    gain_ref, key_ref, value_ref, cos_ref, sin_ref, column_ref, row_ref = refs[n_parts:-2]
+    gain_ref, key_ref, value_ref, cos_ref, sin_ref, owner_ref = refs[n_parts:-2]
     out_ref, total_ref = refs[-2:]
     rows, part_width = parts[0].shape
     key_width = key_ref.shape[1]
-    pages = column_ref.shape[0]
-    earlier = lax.broadcasted_iota(jnp.int32, (pages, pages), 1) < lax.broadcasted_iota(
-        jnp.int32, (pages, pages), 0
-    )
-    same = earlier & (column_ref[...] == row_ref[...])
+    pages = owner_ref.shape[1]
+    down = lax.broadcasted_iota(jnp.int32, (pages, pages), 0)
+    along = lax.broadcasted_iota(jnp.int32, (pages, pages), 1)
+    owners = jnp.broadcast_to(owner_ref[...].astype(jnp.float32), (pages, pages))
+    column = jnp.sum(jnp.where(down == along, owners, 0.0), axis=1, keepdims=True)
+    same = (along < down) & (column == owners)
     rank = jnp.sum(same.astype(jnp.float32), axis=1, keepdims=True)
-    codes = column_ref[...].astype(jnp.float32) * CAP + rank
+    codes = column * CAP + rank
     out_ref[rows:] = jnp.broadcast_to(codes, (pages, 2 * key_width)).astype(jnp.bfloat16)
     squares = jnp.zeros((rows, HD), jnp.float32)
     for part in parts:
@@ -106,7 +107,7 @@
     return pl.pallas_call(
         functools.partial(project_kernel, n_parts, math.gcd(part_width, 1024)),
         out_shape=jax.ShapeDtypeStruct((rows + pages, 2 * key_width), jnp.bfloat16),
-        in_specs=[pl.BlockSpec(memory_space=pltpu.SMEM)] + [vmem] * (n_parts + 7),
+        in_specs=[pl.BlockSpec(memory_space=pltpu.SMEM)] + [vmem] * (n_parts + 6),
         out_specs=vmem,
         scratch_shapes=[pltpu.VMEM((rows, 2 * key_width), jnp.float32)],
         compiler_params=params(),
@@ -124,7 +125,6 @@
         value_weight,
         cosine,
         sine,
-        page_owner.reshape(-1, 1),
         page_owner.reshape(1, -1),
     )
 

time: 114 us -> 113 us (level)
  transfers between devices with their start and end apart: 20 -> 20, of which waited for: 7 -> 7; matrix products, arithmetic and copies ran while one was open for 4% -> 3% of each run, Pallas kernels for 46% -> 47%
where the time goes in v1:
time: 113 us
  Pallas kernels  71.2 us (63%)
  starting transfers between devices  28.3 us (25%)
  waiting for transfers between devices  7.08 us (6%)
  local copies, waits for them, and re-layouts  3.92 us (3%)
  other arithmetic  1.38 us (1%)
    pallas_call x5, Pallas kernels, attend(): pl.pallas_call(functools.partial(attend_kernel, n_blocks, len(held), kv_h...  50.6 us
    ppermute x19, starting transfers between devices, move(): return lax.ppermute(block, 'section', pairs)  27.8 us
    pallas_call x1, Pallas kernels, resident_attention(): pl.pallas_call(functools.partial(resident_kernel, group, pool), out_shape...  8.75 us
    ppermute x19, waiting for transfers between devices, move(): return lax.ppermute(block, 'section', pairs)  7.08 us
    pallas_call x1, Pallas kernels, project(): pl.pallas_call(functools.partial(project_kernel, n_parts, math.gcd(part_w...  5.95 us
    pallas_call x1, Pallas kernels, stage(): pl.pallas_call(functools.partial(stage_kernel, len(arrays)), out_shape=tu...  5.93 us
  transfers between devices with their start and end apart: 20, of which 7 were waited for; matrix products, arithmetic and copies ran while one was open for 3% of the time, Pallas kernels for 47%

profile of v1, /device:TPU:0, one launch (start us, length us, event | category | flops | bytes accessed | tf_op | source)
XLA Modules:
  0.0 112.9 jit_solution(7203295029488271873)
XLA Ops:
  0.6 0.5 collective-permute-start
  1.2 5.9 %stage.1 = (bf16[8192,512]{1,0:T(8,128)(2,1)S(1)}, bf16[8192,512]{1,0:T(8,128)(2,1)S(1)}) custom-call(bf16[8192,512]{1,0:T(8,128)(2,1)} %refs_0_.7, bf16[8192,512]{1,0:T(8,128)(2,1)} %refs_1_.1), custom_call_target="tpu_custom_call" | custom-call | bytes 33554432 | tf_op jit(solution)/shard_map/stage/pallas_call | solution.py:39
  7.1 0.1 pad_add_fusion.1.order_ref
  7.2 0.5 fusion
  7.7 0.1 maximum_multiply_fusion
  7.9 5.9 %project.1.refs_1_ = bf16[272,1024]{1,0:T(8,128)(2,1)S(1)} custom-call(s32[2]{0:T(128)S(1)} %pad_add_fusion.1.order_ref, bf16[256,4096]{1,0:T(8,128)(2,1)S(1)} %copy-done, bf16[256,4096]{1,0:T(8,128)(2,1)S(1)} %collective-permute-done.refs_1_, f32[1,8192]{1,0:T(1,128)S(1)} %bitcast.25, bf16[8192,512]{1,0:T(8,128)(2,1)S(1)} %get-tuple-element.49.refs_3_, ...), custom_call_target="tpu_custom_call" | custom-call | flops 4294967296 | bytes 16777216 | tf_op jit(solution)/shard_map/project/pallas_call | solution.py:107
  13.9 0.7 collective-permute-start.4
  14.6 5.5 %collective-permute-start.3 = (bf16[272,1024]{1,0:T(8,128)(2,1)S(1)}, bf16[272,1024]{1,0:T(8,128)(2,1)S(1)}, u32[]{:S(2)}, u32[]{:S(2)}) collective-permute-start(bf16[272,1024]{1,0:T(8,128)(2,1)S(1)} %project.1.refs_1_), channel_id=1, source_target_pairs={{0,8},{2,10},{4,12},{6,14},{8,0},{10,2},{12,4},{14,6},{16,24},{18,... | collective-permute-start | bytes 1671176 | tf_op jit(solution)/shard_map/ppermute | solution.py:488
  20.1 1.5 %collective-permute-start.2 = (bf16[272,1024]{1,0:T(8,128)(2,1)S(1)}, bf16[272,1024]{1,0:T(8,128)(2,1)S(1)}, u32[]{:S(2)}, u32[]{:S(2)}) collective-permute-start(bf16[272,1024]{1,0:T(8,128)(2,1)S(1)} %project.1.refs_1_), channel_id=1, source_target_pairs={{0,4},{2,6},{4,0},{6,2},{8,12},{10,14},{12,8},{14,10},{16,20},{18,... | collective-permute-start | bytes 1671176 | tf_op jit(solution)/shard_map/ppermute | solution.py:488
  21.6 1.5 %collective-permute-start.1 = (bf16[272,1024]{1,0:T(8,128)(2,1)S(1)}, bf16[272,1024]{1,0:T(8,128)(2,1)S(1)}, u32[]{:S(2)}, u32[]{:S(2)}) collective-permute-start(bf16[272,1024]{1,0:T(8,128)(2,1)S(1)} %project.1.refs_1_), channel_id=1, source_target_pairs={{0,2},{2,0},{4,6},{6,4},{8,10},{10,8},{12,14},{14,12},{16,18},{18,... | collective-permute-start | bytes 1671176 | tf_op jit(solution)/shard_map/ppermute | solution.py:488
  23.1 0.1 stack.120.place_ref
  23.2 0.7 stack.119.slot_ref
  23.9 0.1 pad_add_fusion.2
  23.9 0.7 concatenate.15
  24.6 0.1 copy.13
  24.7 0.7 concatenate.14
  25.5 8.8 %resident.1 = (f32[4,128,128]{2,1,0:T(8,128)}, f32[4,8,128]{2,1,0:T(8,128)}, f32[512,128]{1,0:T(8,128)}) custom-call(s32[16]{0:T(128)} %stack.119.slot_ref, bf16[16,4096]{1,0:T(8,128)(2,1)} %refs_6_.1, bf16[4096,512]{1,0:T(8,128)(2,1)} %bitcast.27, bf16[4096,512]{1,0:T(8,128)(2,1)} %bitcast.28, s32[62,128]{1,0:T(8,128)} %bitcast.29, s32[1,128]{1,0:T(1,128)} %bitcast.30), custom_call_target="tpu_custom_call" | custom-call | flops 1610612736 | bytes 8388608 | tf_op jit(solution)/shard_map/resident/pallas_call | solution.py:232
  34.2 0.3 collective-permute-done.2.refs_3_
  34.5 1.2 %collective-permute-done.1.refs_2_ = bf16[272,1024]{1,0:T(8,128)(2,1)S(1)} collective-permute-done((bf16[272,1024]{1,0:T(8,128)(2,1)S(1)}, bf16[272,1024]{1,0:T(8,128)(2,1)S(1)}, u32[]{:S(2)}, u32[]{:S(2)}) %collective-permute-start.1) | collective-permute-done | bytes 557088 | tf_op jit(solution)/shard_map/ppermute | solution.py:488
  35.8 0.7 collective-permute-start.8
  36.4 0.6 collective-permute-start.6
  37.0 1.5 %collective-permute-start.5 = (bf16[272,1024]{1,0:T(8,128)(2,1)S(1)}, bf16[272,1024]{1,0:T(8,128)(2,1)S(1)}, u32[]{:S(2)}, u32[]{:S(2)}) collective-permute-start(bf16[272,1024]{1,0:T(8,128)(2,1)S(1)} %collective-permute-done.2.refs_3_), channel_id=1, source_target_pairs={{0,2},{2,0},{4,6},{6,4},{8,10},{10,8},{12,14},{14,12},{16,18},{18,... | collective-permute-start | bytes 1671176 | tf_op jit(solution)/shard_map/ppermute | solution.py:488
  38.5 1.5 %collective-permute-start.7 = (bf16[272,1024]{1,0:T(8,128)(2,1)S(1)}, bf16[272,1024]{1,0:T(8,128)(2,1)S(1)}, u32[]{:S(2)}, u32[]{:S(2)}) collective-permute-start(bf16[272,1024]{1,0:T(8,128)(2,1)S(1)} %collective-permute-done.4), channel_id=1, source_target_pairs={{8,0},{10,2},{12,4},{14,6},{16,24},{18,26},{20,28},{22,30},{9,1},{... | collective-permute-start | bytes 1671176 | tf_op jit(solution)/shard_map/ppermute | solution.py:488
  40.0 1.6 %copy-done.4 = bf16[256,4096]{1,0:T(8,128)(2,1)S(1)} copy-done((bf16[256,4096]{1,0:T(8,128)(2,1)S(1)}, bf16[256,4096]{1,0:T(8,128)(2,1)}, u32[]{:S(2)}) %copy-start.4) | copy-done | bytes 2097176
  41.6 10.8 %attend.5 = (f32[4,128,2048]{2,1,0:T(8,128)S(1)}, f32[4,8,2048]{2,1,0:T(8,128)S(1)}, bf16[4,128,256]{2,1,0:T(8,128)(2,1)S(1)}) custom-call(s32[5]{0:T(128)S(1)} %stack.120.place_ref, bf16[256,4096]{1,0:T(8,128)(2,1)S(1)} %copy-done.4, bf16[272,1024]{1,0:T(8,128)(2,1)S(1)} %project.1.refs_1_, bf16[272,1024]{1,0:T(8,128)(2,1)S(1)} %collective-permute-done.1.refs_2_, ...), custom_call_target="tpu_custom_call" | custom-call | flops 6442450944 | bytes 12582912 | tf_op jit(solution)/shard_map/attend/pallas_call | solution.py:418
  52.4 0.8 collective-permute-done.7
  53.2 0.7 collective-permute-start.12
  54.0 4.2 %collective-permute-start.11 = (bf16[272,1024]{1,0:T(8,128)(2,1)S(1)}, bf16[272,1024]{1,0:T(8,128)(2,1)S(1)}, u32[]{:S(2)}, u32[]{:S(2)}) collective-permute-start(bf16[272,1024]{1,0:T(8,128)(2,1)S(1)} %broadcast_select_fusion.4), channel_id=1, source_target_pairs={{0,8},{2,10},{4,12},{6,14},{8,0},{10,2},{12,4},{14,6},{16,24},{18,... | collective-permute-start | bytes 1671176 | tf_op jit(solution)/shard_map/ppermute | solution.py:488
  58.1 0.1 broadcast_select_fusion.5.refs_3_
  58.2 1.6 %collective-permute-start.10 = (bf16[272,1024]{1,0:T(8,128)(2,1)S(1)}, bf16[272,1024]{1,0:T(8,128)(2,1)S(1)}, u32[]{:S(2)}, u32[]{:S(2)}) collective-permute-start(bf16[272,1024]{1,0:T(8,128)(2,1)S(1)} %broadcast_select_fusion.5.refs_3_), channel_id=1, source_target_pairs={{0,4},{2,6},{4,0},{6,2},{8,12},{10,14},{12,8},{14,10},{16,20},{18,... | collective-permute-start | bytes 1671176 | tf_op jit(solution)/shard_map/ppermute | solution.py:488
  59.8 0.5 collective-permute-start.9
  60.3 0.1 pad_add_fusion.4.place_ref
  60.4 9.1 %attend.6 = (f32[4,128,2048]{2,1,0:T(8,128)S(1)}, f32[4,8,2048]{2,1,0:T(8,128)S(1)}, bf16[4,96,256]{2,1,0:T(8,128)(2,1)S(1)}) custom-call(s32[4]{0:T(128)S(1)} %get-tuple-element.99.place_ref, bf16[256,4096]{1,0:T(8,128)(2,1)S(1)} %copy-done.4, bf16[272,1024]{1,0:T(8,128)(2,1)S(1)} %collective-permute-done.5.refs_1_, ...), custom_call_target="tpu_custom_call" | custom-call | flops 4831838208 | bytes 12582912 | tf_op jit(solution)/shard_map/attend/pallas_call | solution.py:418
  69.5 1.1 collective-permute-done.10.refs_2_
  70.6 1.1 %collective-permute-done.9.refs_1_ = bf16[272,1024]{1,0:T(8,128)(2,1)S(1)} collective-permute-done((bf16[272,1024]{1,0:T(8,128)(2,1)S(1)}, bf16[272,1024]{1,0:T(8,128)(2,1)S(1)}, u32[]{:S(2)}, u32[]{:S(2)}) %collective-permute-start.9) | collective-permute-done | bytes 557088 | tf_op jit(solution)/shard_map/ppermute | solution.py:488
  71.7 0.7 collective-permute-start.16
  72.5 0.7 collective-permute-start.14
  73.1 0.5 collective-permute-start.13
  73.7 1.5 %collective-permute-start.15 = (bf16[272,1024]{1,0:T(8,128)(2,1)S(1)}, bf16[272,1024]{1,0:T(8,128)(2,1)S(1)}, u32[]{:S(2)}, u32[]{:S(2)}) collective-permute-start(bf16[272,1024]{1,0:T(8,128)(2,1)S(1)} %collective-permute-done.12), channel_id=1, source_target_pairs={{8,0},{10,2},{12,4},{14,6},{16,24},{18,26},{20,28},{22,30},{9,1},{... | collective-permute-start | bytes 1671176 | tf_op jit(solution)/shard_map/ppermute | solution.py:488
  75.2 0.1 pad_add_fusion.place_ref
  75.3 9.2 %attend.7 = (f32[4,128,2048]{2,1,0:T(8,128)S(1)}, f32[4,8,2048]{2,1,0:T(8,128)S(1)}, bf16[4,96,256]{2,1,0:T(8,128)(2,1)S(1)}) custom-call(s32[4]{0:T(128)S(1)} %get-tuple-element.100.place_ref, bf16[256,4096]{1,0:T(8,128)(2,1)S(1)} %copy-done.4, bf16[272,1024]{1,0:T(8,128)(2,1)S(1)} %collective-permute-done.9.refs_1_, ...), custom_call_target="tpu_custom_call" | custom-call | flops 4831838208 | bytes 12582912 | tf_op jit(solution)/shard_map/attend/pallas_call | solution.py:418
  84.5 1.6 %collective-permute-done.15 = bf16[272,1024]{1,0:T(8,128)(2,1)S(1)} collective-permute-done((bf16[272,1024]{1,0:T(8,128)(2,1)S(1)}, bf16[272,1024]{1,0:T(8,128)(2,1)S(1)}, u32[]{:S(2)}, u32[]{:S(2)}) %collective-permute-start.15) | collective-permute-done | bytes 557088 | tf_op jit(solution)/shard_map/ppermute | solution.py:488
  86.1 1.5 %collective-permute-start.17 = (bf16[272,1024]{1,0:T(8,128)(2,1)S(1)}, bf16[272,1024]{1,0:T(8,128)(2,1)S(1)}, u32[]{:S(2)}, u32[]{:S(2)}) collective-permute-start(bf16[272,1024]{1,0:T(8,128)(2,1)S(1)} %broadcast_select_fusion.3.refs_3_), channel_id=1, source_target_pairs={{0,2},{2,0},{4,6},{6,4},{8,10},{10,8},{12,14},{14,12},{16,18},{18,... | collective-permute-start | bytes 1671176 | tf_op jit(solution)/shard_map/ppermute | solution.py:488
  87.6 1.3 %collective-permute-start.18 = (bf16[272,1024]{1,0:T(8,128)(2,1)S(1)}, bf16[272,1024]{1,0:T(8,128)(2,1)S(1)}, u32[]{:S(2)}, u32[]{:S(2)}) collective-permute-start(bf16[272,1024]{1,0:T(8,128)(2,1)S(1)} %collective-permute-done.9.refs_1_), channel_id=1, source_target_pairs={{0,4},{2,6},{4,0},{6,2},{8,12},{10,14},{12,8},{14,10},{16,20},{18,... | collective-permute-start | bytes 1671176 | tf_op jit(solution)/shard_map/ppermute | solution.py:488
  88.9 1.3 %collective-permute-start.19 = (bf16[272,1024]{1,0:T(8,128)(2,1)S(1)}, bf16[272,1024]{1,0:T(8,128)(2,1)S(1)}, u32[]{:S(2)}, u32[]{:S(2)}) collective-permute-start(bf16[272,1024]{1,0:T(8,128)(2,1)S(1)} %collective-permute-done.16), channel_id=1, source_target_pairs={{8,0},{10,2},{12,4},{14,6},{16,24},{18,26},{20,28},{22,30},{9,1},{... | collective-permute-start | bytes 1671176 | tf_op jit(solution)/shard_map/ppermute | solution.py:488
  90.3 9.1 %attend.8 = (f32[4,128,2048]{2,1,0:T(8,128)S(1)}, f32[4,8,2048]{2,1,0:T(8,128)S(1)}, bf16[4,96,256]{2,1,0:T(8,128)(2,1)S(1)}) custom-call(s32[4]{0:T(128)S(1)} %pad_add_fusion.4.place_ref, bf16[256,4096]{1,0:T(8,128)(2,1)S(1)} %copy-done.4, bf16[272,1024]{1,0:T(8,128)(2,1)S(1)} %collective-permute-done.13.refs_1_, ...), custom_call_target="tpu_custom_call" | custom-call | flops 4831838208 | bytes 12582912 | tf_op jit(solution)/shard_map/attend/pallas_call | solution.py:418
  99.4 0.9 collective-permute-done.19
  100.5 12.4 %attend.9 = (bf16[256,4096]{1,0:T(8,128)(2,1)}, bf16[16,4096]{1,0:T(8,128)(2,1)}) custom-call(s32[4]{0:T(128)S(1)} %pad_add_fusion.place_ref, bf16[256,4096]{1,0:T(8,128)(2,1)S(1)} %copy-done.4, bf16[272,1024]{1,0:T(8,128)(2,1)S(1)} %collective-permute-done.17.refs_1_, bf16[272,1024]{1,0:T(8,128)(2,1)S(1)} %broadcast_select_fusion.1.refs_2_, ...), custom_call_target="tpu_custom_call" | custom-call | flops 4831838208 | bytes 12582912 | tf_op jit(solution)/shard_map/attend/pallas_call | solution.py:418
  (39 shorter events, 0.4 us)
Async XLA Ops:
  0.6 7.3 %collective-permute-start = (bf16[256,4096]{1,0:T(8,128)(2,1)}, bf16[256,4096]{1,0:T(8,128)(2,1)S(1)}, u32[]{:S(2)}, u32[]{:S(2)}) collective-permute-start(bf16[256,4096]{1,0:T(8,128)(2,1)} %refs_0_.8), channel_id=1, source_target_pairs={{0,1},{1,0},{2,3},{3,2},{4,5},{5,4},{6,7},{7,6},{8,9},{9,8},{10,11... | collective-permute-start | bytes 6291464 | tf_op jit(solution)/shard_map/ppermute | solution.py:552
  1.1 6.7 %copy-start = (bf16[256,4096]{1,0:T(8,128)(2,1)S(1)}, bf16[256,4096]{1,0:T(8,128)(2,1)}, u32[]{:S(2)}) copy-start(bf16[256,4096]{1,0:T(8,128)(2,1)} %refs_0_.8) | copy-start | bytes 6291460
  1.2 6.8 %copy-start.2 = (f32[8192]{0:T(1024)S(1)}, f32[8192]{0:T(1024)}, u32[]{:S(2)}) copy-start(f32[8192]{0:T(1024)} %param.12) | copy-start | bytes 98308
  1.2 6.8 %copy-start.3 = (s32[16]{0:T(128)S(1)}, s32[16]{0:T(128)}, u32[]{:S(2)}) copy-start(s32[16]{0:T(128)} %param.19) | copy-start | bytes 196
  7.9 16.0 %copy-start.8 = (s32[16]{0:T(128)S(1)}, s32[16]{0:T(128)}, u32[]{:S(2)}) copy-start(s32[16]{0:T(128)} %param.21) | copy-start | bytes 196
  7.9 16.7 %copy-start.9 = (s32[16,62]{1,0:T(8,128)S(1)}, s32[16,62]{1,0:T(8,128)}, u32[]{:S(2)}) copy-start(s32[16,62]{1,0:T(8,128)} %param.20) | copy-start | bytes 11908
  13.9 20.3 %collective-permute-start.4 = (bf16[272,1024]{1,0:T(8,128)(2,1)S(1)}, bf16[272,1024]{1,0:T(8,128)(2,1)S(1)}, u32[]{:S(2)}, u32[]{:S(2)}) collective-permute-start(bf16[272,1024]{1,0:T(8,128)(2,1)S(1)} %project.1.refs_1_), channel_id=1, source_target_pairs={{8,16},{10,18},{12,20},{14,22},{16,8},{18,10},{20,12},{22,14},{9,1... | collective-permute-start | bytes 1671176 | tf_op jit(solution)/shard_map/ppermute | solution.py:488
  14.6 19.6 %collective-permute-start.3 = (bf16[272,1024]{1,0:T(8,128)(2,1)S(1)}, bf16[272,1024]{1,0:T(8,128)(2,1)S(1)}, u32[]{:S(2)}, u32[]{:S(2)}) collective-permute-start(bf16[272,1024]{1,0:T(8,128)(2,1)S(1)} %project.1.refs_1_), channel_id=1, source_target_pairs={{0,8},{2,10},{4,12},{6,14},{8,0},{10,2},{12,4},{14,6},{16,24},{18,... | collective-permute-start | bytes 1671176 | tf_op jit(solution)/shard_map/ppermute | solution.py:488
  20.1 14.4 %collective-permute-start.2 = (bf16[272,1024]{1,0:T(8,128)(2,1)S(1)}, bf16[272,1024]{1,0:T(8,128)(2,1)S(1)}, u32[]{:S(2)}, u32[]{:S(2)}) collective-permute-start(bf16[272,1024]{1,0:T(8,128)(2,1)S(1)} %project.1.refs_1_), channel_id=1, source_target_pairs={{0,4},{2,6},{4,0},{6,2},{8,12},{10,14},{12,8},{14,10},{16,20},{18,... | collective-permute-start | bytes 1671176 | tf_op jit(solution)/shard_map/ppermute | solution.py:488
  21.6 14.2 %collective-permute-start.1 = (bf16[272,1024]{1,0:T(8,128)(2,1)S(1)}, bf16[272,1024]{1,0:T(8,128)(2,1)S(1)}, u32[]{:S(2)}, u32[]{:S(2)}) collective-permute-start(bf16[272,1024]{1,0:T(8,128)(2,1)S(1)} %project.1.refs_1_), channel_id=1, source_target_pairs={{0,2},{2,0},{4,6},{6,4},{8,10},{10,8},{12,14},{14,12},{16,18},{18,... | collective-permute-start | bytes 1671176 | tf_op jit(solution)/shard_map/ppermute | solution.py:488
  35.8 17.5 %collective-permute-start.8 = (bf16[272,1024]{1,0:T(8,128)(2,1)S(1)}, bf16[272,1024]{1,0:T(8,128)(2,1)S(1)}, u32[]{:S(2)}, u32[]{:S(2)}) collective-permute-start(bf16[272,1024]{1,0:T(8,128)(2,1)S(1)} %collective-permute-done.3.refs_4_), channel_id=1, source_target_pairs={{8,16},{10,18},{12,20},{14,22},{16,8},{18,10},{20,12},{22,14},{9,1... | collective-permute-start | bytes 1671176 | tf_op jit(solution)/shard_map/ppermute | solution.py:488
  36.4 16.8 %collective-permute-start.6 = (bf16[272,1024]{1,0:T(8,128)(2,1)S(1)}, bf16[272,1024]{1,0:T(8,128)(2,1)S(1)}, u32[]{:S(2)}, u32[]{:S(2)}) collective-permute-start(bf16[272,1024]{1,0:T(8,128)(2,1)S(1)} %collective-permute-done.3.refs_4_), channel_id=1, source_target_pairs={{0,4},{2,6},{4,0},{6,2},{8,12},{10,14},{12,8},{14,10},{16,20},{18,... | collective-permute-start | bytes 1671176 | tf_op jit(solution)/shard_map/ppermute | solution.py:488
  37.0 15.4 %collective-permute-start.5 = (bf16[272,1024]{1,0:T(8,128)(2,1)S(1)}, bf16[272,1024]{1,0:T(8,128)(2,1)S(1)}, u32[]{:S(2)}, u32[]{:S(2)}) collective-permute-start(bf16[272,1024]{1,0:T(8,128)(2,1)S(1)} %collective-permute-done.2.refs_3_), channel_id=1, source_target_pairs={{0,2},{2,0},{4,6},{6,4},{8,10},{10,8},{12,14},{14,12},{16,18},{18,... | collective-permute-start | bytes 1671176 | tf_op jit(solution)/shard_map/ppermute | solution.py:488
  38.5 14.7 %collective-permute-start.7 = (bf16[272,1024]{1,0:T(8,128)(2,1)S(1)}, bf16[272,1024]{1,0:T(8,128)(2,1)S(1)}, u32[]{:S(2)}, u32[]{:S(2)}) collective-permute-start(bf16[272,1024]{1,0:T(8,128)(2,1)S(1)} %collective-permute-done.4), channel_id=1, source_target_pairs={{8,0},{10,2},{12,4},{14,6},{16,24},{18,26},{20,28},{22,30},{9,1},{... | collective-permute-start | bytes 1671176 | tf_op jit(solution)/shard_map/ppermute | solution.py:488
  40.0 1.6 %copy-start.4 = (bf16[256,4096]{1,0:T(8,128)(2,1)S(1)}, bf16[256,4096]{1,0:T(8,128)(2,1)}, u32[]{:S(2)}) copy-start(bf16[256,4096]{1,0:T(8,128)(2,1)} %refs_0_.13) | copy-start | bytes 6291460
  53.2 18.5 %collective-permute-start.12 = (bf16[272,1024]{1,0:T(8,128)(2,1)S(1)}, bf16[272,1024]{1,0:T(8,128)(2,1)S(1)}, u32[]{:S(2)}, u32[]{:S(2)}) collective-permute-start(bf16[272,1024]{1,0:T(8,128)(2,1)S(1)} %collective-permute-done.5.refs_1_), channel_id=1, source_target_pairs={{8,16},{10,18},{12,20},{14,22},{16,8},{18,10},{20,12},{22,14},{9,1... | collective-permute-start | bytes 1671176 | tf_op jit(solution)/shard_map/ppermute | solution.py:488
  54.0 15.5 %collective-permute-start.11 = (bf16[272,1024]{1,0:T(8,128)(2,1)S(1)}, bf16[272,1024]{1,0:T(8,128)(2,1)S(1)}, u32[]{:S(2)}, u32[]{:S(2)}) collective-permute-start(bf16[272,1024]{1,0:T(8,128)(2,1)S(1)} %broadcast_select_fusion.4), channel_id=1, source_target_pairs={{0,8},{2,10},{4,12},{6,14},{8,0},{10,2},{12,4},{14,6},{16,24},{18,... | collective-permute-start | bytes 1671176 | tf_op jit(solution)/shard_map/ppermute | solution.py:488
  58.2 12.4 %collective-permute-start.10 = (bf16[272,1024]{1,0:T(8,128)(2,1)S(1)}, bf16[272,1024]{1,0:T(8,128)(2,1)S(1)}, u32[]{:S(2)}, u32[]{:S(2)}) collective-permute-start(bf16[272,1024]{1,0:T(8,128)(2,1)S(1)} %broadcast_select_fusion.5.refs_3_), channel_id=1, source_target_pairs={{0,4},{2,6},{4,0},{6,2},{8,12},{10,14},{12,8},{14,10},{16,20},{18,... | collective-permute-start | bytes 1671176 | tf_op jit(solution)/shard_map/ppermute | solution.py:488
  59.8 11.9 %collective-permute-start.9 = (bf16[272,1024]{1,0:T(8,128)(2,1)S(1)}, bf16[272,1024]{1,0:T(8,128)(2,1)S(1)}, u32[]{:S(2)}, u32[]{:S(2)}) collective-permute-start(bf16[272,1024]{1,0:T(8,128)(2,1)S(1)} %collective-permute-done.3.refs_4_), channel_id=1, source_target_pairs={{0,2},{2,0},{4,6},{6,4},{8,10},{10,8},{12,14},{14,12},{16,18},{18,... | collective-permute-start | bytes 1671176 | tf_op jit(solution)/shard_map/ppermute | solution.py:488
  71.7 14.4 %collective-permute-start.16 = (bf16[272,1024]{1,0:T(8,128)(2,1)S(1)}, bf16[272,1024]{1,0:T(8,128)(2,1)S(1)}, u32[]{:S(2)}, u32[]{:S(2)}) collective-permute-start(bf16[272,1024]{1,0:T(8,128)(2,1)S(1)} %collective-permute-done.11), channel_id=1, source_target_pairs={{8,16},{10,18},{12,20},{14,22},{16,8},{18,10},{20,12},{22,14},{9,1... | collective-permute-start | bytes 1671176 | tf_op jit(solution)/shard_map/ppermute | solution.py:488
  72.5 12.0 %collective-permute-start.14 = (bf16[272,1024]{1,0:T(8,128)(2,1)S(1)}, bf16[272,1024]{1,0:T(8,128)(2,1)S(1)}, u32[]{:S(2)}, u32[]{:S(2)}) collective-permute-start(bf16[272,1024]{1,0:T(8,128)(2,1)S(1)} %broadcast_select_fusion.3.refs_3_), channel_id=1, source_target_pairs={{0,4},{2,6},{4,0},{6,2},{8,12},{10,14},{12,8},{14,10},{16,20},{18,... | collective-permute-start | bytes 1671176 | tf_op jit(solution)/shard_map/ppermute | solution.py:488
  73.1 11.3 %collective-permute-start.13 = (bf16[272,1024]{1,0:T(8,128)(2,1)S(1)}, bf16[272,1024]{1,0:T(8,128)(2,1)S(1)}, u32[]{:S(2)}, u32[]{:S(2)}) collective-permute-start(bf16[272,1024]{1,0:T(8,128)(2,1)S(1)} %broadcast_select_fusion.5.refs_3_), channel_id=1, source_target_pairs={{0,2},{2,0},{4,6},{6,4},{8,10},{10,8},{12,14},{14,12},{16,18},{18,... | collective-permute-start | bytes 1671176 | tf_op jit(solution)/shard_map/ppermute | solution.py:488
  73.7 12.4 %collective-permute-start.15 = (bf16[272,1024]{1,0:T(8,128)(2,1)S(1)}, bf16[272,1024]{1,0:T(8,128)(2,1)S(1)}, u32[]{:S(2)}, u32[]{:S(2)}) collective-permute-start(bf16[272,1024]{1,0:T(8,128)(2,1)S(1)} %collective-permute-done.12), channel_id=1, source_target_pairs={{8,0},{10,2},{12,4},{14,6},{16,24},{18,26},{20,28},{22,30},{9,1},{... | collective-permute-start | bytes 1671176 | tf_op jit(solution)/shard_map/ppermute | solution.py:488
  86.1 13.3 %collective-permute-start.17 = (bf16[272,1024]{1,0:T(8,128)(2,1)S(1)}, bf16[272,1024]{1,0:T(8,128)(2,1)S(1)}, u32[]{:S(2)}, u32[]{:S(2)}) collective-permute-start(bf16[272,1024]{1,0:T(8,128)(2,1)S(1)} %broadcast_select_fusion.3.refs_3_), channel_id=1, source_target_pairs={{0,2},{2,0},{4,6},{6,4},{8,10},{10,8},{12,14},{14,12},{16,18},{18,... | collective-permute-start | bytes 1671176 | tf_op jit(solution)/shard_map/ppermute | solution.py:488
  87.6 11.8 %collective-permute-start.18 = (bf16[272,1024]{1,0:T(8,128)(2,1)S(1)}, bf16[272,1024]{1,0:T(8,128)(2,1)S(1)}, u32[]{:S(2)}, u32[]{:S(2)}) collective-permute-start(bf16[272,1024]{1,0:T(8,128)(2,1)S(1)} %collective-permute-done.9.refs_1_), channel_id=1, source_target_pairs={{0,4},{2,6},{4,0},{6,2},{8,12},{10,14},{12,8},{14,10},{16,20},{18,... | collective-permute-start | bytes 1671176 | tf_op jit(solution)/shard_map/ppermute | solution.py:488
  88.9 11.4 %collective-permute-start.19 = (bf16[272,1024]{1,0:T(8,128)(2,1)S(1)}, bf16[272,1024]{1,0:T(8,128)(2,1)S(1)}, u32[]{:S(2)}, u32[]{:S(2)}) collective-permute-start(bf16[272,1024]{1,0:T(8,128)(2,1)S(1)} %collective-permute-done.16), channel_id=1, source_target_pairs={{8,0},{10,2},{12,4},{14,6},{16,24},{18,26},{20,28},{22,30},{9,1},{... | collective-permute-start | bytes 1671176 | tf_op jit(solution)/shard_map/ppermute | solution.py:488
  90.2 10.2 %copy-start.1 = (bf16[16,4096]{1,0:T(8,128)(2,1)S(1)}, bf16[16,4096]{1,0:T(8,128)(2,1)}, u32[]{:S(2)}) copy-start(bf16[16,4096]{1,0:T(8,128)(2,1)} %refs_6_.1) | copy-start | bytes 393220
  90.3 10.2 %copy-start.5 = (f32[4,128,128]{2,1,0:T(8,128)S(1)}, f32[4,128,128]{2,1,0:T(8,128)}, u32[]{:S(2)}) copy-start(f32[4,128,128]{2,1,0:T(8,128)} %get-tuple-element.54.refs_7_) | copy-start | bytes 786436
  90.3 10.2 %copy-start.6 = (f32[512,128]{1,0:T(8,128)S(1)}, f32[512,128]{1,0:T(8,128)}, u32[]{:S(2)}) copy-start(f32[512,128]{1,0:T(8,128)} %get-tuple-element.56.refs_9_) | copy-start | bytes 786436
  90.3 10.2 %copy-start.7 = (f32[4,8,128]{2,1,0:T(8,128)S(1)}, f32[4,8,128]{2,1,0:T(8,128)}, u32[]{:S(2)}) copy-start(f32[4,8,128]{2,1,0:T(8,128)} %get-tuple-element.55.refs_8_) | copy-start | bytes 49156
